TPU v7x, 32 devices: a whole 2x2x4 slice. The times are simulated.
32 devices in a mesh: frame: 16 (over z, y, core), pix: 2 (over x).
Axes of the slice: x: 2, y: 2, z: 4, core: 2. Of those that a mesh axis runs over, the one named last changes fastest.
Arguments:
- library: float32 [6144, 3072], P('frame', 'pix'), may hold values from -5000 to 5000
- annulus: int32 [1536], P('pix'), may hold values from 0 to 1535, as said below
Outputs:
- gram: float32 [6144, 6144], P('frame', 'pix')
Inputs may be any that keep to these rules, and one draw needn't show every extreme that they name: `annulus`: within each aligned block of 768 entries the values are distinct and rising, and each block holds both 0 and 1535.
All inputs are finite; a program needn't handle non-finite values.
Results may differ from a plain program's by a relative error of at most 0.000065.
Values sent between devices are 32-bit elements; how exact they have to be, the bound alone decides.
No kernel may reach another device: no remote copies, remote signals or barrier semaphores. Data moves between devices by JAX's collectives and lax.ppermute only.
A program may use at most 128 MiB of HBM per device.

v0:
```python
import functools

import jax
import jax.numpy as jnp
from jax import lax
from jax.experimental import pallas as pl
from jax.experimental.pallas import tpu as pltpu
from jax.sharding import PartitionSpec as P

PIX = 1536
EPS = 1e-06
CHUNKS = (128, 128, 128)
STAT_ROWS = 8
SMALL, VMEM = 6 << 20, 28 << 20
FREE = pl.CostEstimate(flops=1, bytes_accessed=1, transcendentals=0)
F32, BF16 = jnp.float32, jnp.bfloat16


def split(a):
    high = a.astype(BF16)
    return high, (a - high.astype(F32)).astype(BF16)


def pick_kernel(annulus_ref, library_ref, place_ref, whole_ref, *piece_refs):
    rows, band = library_ref.shape
    pix = annulus_ref.shape[0]
    frame, x = lax.axis_index("frame"), lax.axis_index("pix")
    z = frame // 4
    for j in range(2):
        place_ref[j] = jnp.where((z + 4 - j) % 4 // 2 == x, 1, 0)
        for s in range(4):
            place_ref[2 + 4 * j + s] = (z + 4 - j) % 2 * 4 + ((frame % 4) ^ s)
    tile = 256
    width = band - pix + tile
    columns = []
    for start in range(0, pix, tile):
        a = library_ref[:, start : start + width]
        high, rest = split(a)
        mid, low = split(a - high.astype(F32))
        where = annulus_ref[start : start + tile].reshape(1, tile) - start
        one_hot = jnp.where(
            lax.broadcasted_iota(jnp.int32, (width, tile), 0) == where, 1.0, 0.0
        ).astype(BF16)
        parts = jnp.dot(
            jnp.concatenate([high, mid, low], axis=0),
            one_hot,
            preferred_element_type=F32,
        )
        columns.append(
            parts[:rows] + parts[rows : 2 * rows] + parts[2 * rows :]
        )
    picked = jnp.concatenate(columns, axis=1)
    mean = jnp.sum(picked, axis=1, keepdims=True) / pix
    centered = picked - mean
    shift = jnp.sum(centered, axis=1, keepdims=True) / pix
    centered = centered - shift
    mean = mean + shift
    squares = jnp.sum(centered * centered, axis=1, keepdims=True)
    as_row = [
        jnp.transpose(jnp.broadcast_to(v, (rows, 128)))[:STAT_ROWS]
        for v in (mean, squares)
    ]
    stat = jnp.concatenate(as_row, axis=1)
    whole_ref[:rows], whole_ref[rows:] = centered, stat
    start = 0
    for ref, count in zip(piece_refs, CHUNKS):
        ref[:count] = centered[start : start + count]
        start += count
    piece_refs[0][CHUNKS[0] :] = stat


def pick(library, annulus):
    rows = library.shape[0]
    pix = annulus.shape[0]
    counts = [rows + STAT_ROWS, CHUNKS[0] + STAT_ROWS, *CHUNKS[1:]]
    return pl.pallas_call(
        pick_kernel,
        out_shape=[jax.ShapeDtypeStruct((10,), jnp.int32)]
        + [jax.ShapeDtypeStruct((count, pix), F32) for count in counts],
        out_specs=[pl.BlockSpec(memory_space=pltpu.SMEM)]
        + [pl.BlockSpec(memory_space=pltpu.VMEM)] * len(counts),
        compiler_params=pltpu.CompilerParams(vmem_limit_bytes=VMEM),
        cost_estimate=FREE,
        name="pick",
    )(annulus, library)


def cut_kernel(whole_ref, *refs):
    out_refs = refs[-len(CHUNKS) :]
    rows = whole_ref.shape[0] - STAT_ROWS
    start = 0
    for ref, count in zip(out_refs, CHUNKS):
        ref[:count] = whole_ref[start : start + count]
        start += count
    out_refs[0][CHUNKS[0] :] = whole_ref[rows:]


def cut(whole, after):
    pix = whole.shape[1]
    counts = [CHUNKS[0] + STAT_ROWS, *CHUNKS[1:]]
    vmem = pl.BlockSpec(memory_space=pltpu.VMEM)
    return pl.pallas_call(
        cut_kernel,
        in_specs=[vmem] + [pl.BlockSpec(memory_space=pl.ANY)] * len(after),
        out_specs=[vmem] * len(counts),
        out_shape=[jax.ShapeDtypeStruct((count, pix), F32) for count in counts],
        compiler_params=pltpu.CompilerParams(vmem_limit_bytes=SMALL),
        cost_estimate=FREE,
        name="cut",
    )(whole, *after)


def choose_kernel(j, first_ref, a_ref, b_ref, *refs):
    keep_ref, send_ref = refs[-2:]
    first = first_ref[j] == 1
    a, b = a_ref[...], b_ref[...]
    keep_ref[...] = jnp.where(first, a, b)
    send_ref[...] = jnp.where(first, b, a)


def choose(j, spots, a, b, after):
    vmem = pl.BlockSpec(memory_space=pltpu.VMEM)
    return pl.pallas_call(
        functools.partial(choose_kernel, j),
        in_specs=[pl.BlockSpec(memory_space=pltpu.SMEM), vmem, vmem]
        + [pl.BlockSpec(memory_space=pl.ANY)] * len(after),
        out_specs=[vmem] * 2,
        out_shape=[jax.ShapeDtypeStruct(a.shape, a.dtype)] * 2,
        compiler_params=pltpu.CompilerParams(vmem_limit_bytes=SMALL),
        cost_estimate=FREE,
        name="choose",
    )(spots, a, b, *after)


def pair_kernel(a_ref, b_ref, *refs):
    refs[-1][0], refs[-1][1] = a_ref[...], b_ref[...]


def pair(a, b, after):
    vmem = pl.BlockSpec(memory_space=pltpu.VMEM)
    return pl.pallas_call(
        pair_kernel,
        in_specs=[vmem] * 2 + [pl.BlockSpec(memory_space=pl.ANY)] * len(after),
        out_specs=vmem,
        out_shape=jax.ShapeDtypeStruct((2,) + a.shape, a.dtype),
        compiler_params=pltpu.CompilerParams(vmem_limit_bytes=SMALL),
        cost_estimate=FREE,
        name="pair",
    )(a, b, *after)


def normalize(a, b, a_stat, b_stat, start):
    count, pix = a.shape
    rows = a_stat.shape[1] // 2
    mean = slice(start, start + count)
    squares = slice(rows + start, rows + start + count)
    gap = (a_stat[:, mean] - b_stat[:, mean]) / 2
    total = a_stat[:, squares] + b_stat[:, squares] + (2 * pix) * (gap * gap)
    scale = 1 / jnp.sqrt(total + EPS)
    gap, scale = [
        jnp.transpose(jnp.broadcast_to(v, (128, count)))[:, :1] for v in (gap, scale)
    ]
    return jnp.concatenate([(a + gap) * scale, (b - gap) * scale], axis=1)


def rows_kernel(a_ref, b_ref, out_ref):
    rows = a_ref.shape[0] - STAT_ROWS
    unit = normalize(
        a_ref[:rows], b_ref[:rows], a_ref[rows : rows + 1], b_ref[rows : rows + 1], 0
    )
    out_ref[:rows], out_ref[rows:] = split(unit)


def unit_rows(a, b):
    rows, pix = a.shape[0] - STAT_ROWS, a.shape[1]
    return pl.pallas_call(
        rows_kernel,
        out_shape=jax.ShapeDtypeStruct((2 * rows, 2 * pix), BF16),
        compiler_params=pltpu.CompilerParams(vmem_limit_bytes=12 << 20),
        cost_estimate=FREE,
        name="unit_rows",
    )(a, b)


def product_kernel(start, count, *refs):
    rows_refs, refs = refs[:2], refs[2:]
    keep, received, pair = refs[:3]
    columns = [keep[...], received[...], pair[0], pair[1]]
    if start == 0:
        stats = [a[count : count + 1] for a in columns]
    else:
        stats = [refs[3][0:1], refs[4][0:1], refs[5][0, 0:1], refs[5][1, 0:1]]
    outs = refs[-2:]
    unit = jnp.concatenate(
        [
            normalize(
                columns[c][:count], columns[c + 1][:count], stats[c], stats[c + 1], start
            )
            for c in (0, 2)
        ],
        axis=0,
    )
    high, low = split(unit)
    dot = functools.partial(
        lax.dot_general,
        dimension_numbers=(((1,), (1,)), ((), ())),
        preferred_element_type=F32,
    )
    for rows_ref, out_ref in zip(rows_refs, outs):
        rows = rows_ref.shape[0] // 2
        both = dot(rows_ref[...], high)
        out_ref[...] = both[:rows] + (both[rows:] + dot(rows_ref[:rows], low))


def product(i, near, far, columns, first, after):
    double, depth = near.shape
    start, count = sum(CHUNKS[:i]), CHUNKS[i]
    vmem = pl.BlockSpec(memory_space=pltpu.VMEM)
    in_specs = [vmem] * 5
    operands = [near, far, *columns]
    if i:
        at, pix = CHUNKS[0] // STAT_ROWS, depth // 2
        in_specs += [pl.BlockSpec((STAT_ROWS, pix), lambda i: (at, 0))] * 2
        in_specs.append(pl.BlockSpec((2, STAT_ROWS, pix), lambda i: (0, at, 0)))
        operands += first
    in_specs += [pl.BlockSpec(memory_space=pl.ANY)] * len(after)
    operands += after
    out = jax.ShapeDtypeStruct((double // 2, 2 * count), F32)
    return pl.pallas_call(
        functools.partial(product_kernel, start, count),
        grid=(1,),
        in_specs=in_specs,
        out_specs=[vmem] * 2,
        out_shape=[out] * 2,
        compiler_params=pltpu.CompilerParams(vmem_limit_bytes=16 << 20),
        cost_estimate=FREE,
        name="product",
    )(*operands)


def place_kernel(at_ref, *refs):
    out_ref = refs[-1]
    n = (len(refs) - 1) // 2
    for side in range(2):

        @pl.when(pl.program_id(0) // 2 == side)
        def _():
            parts = [ref[...] for ref in refs[side * n : side * n + n]]
            out_ref[...] = parts[0] if n == 1 else jnp.concatenate(parts, axis=1)


def place(j, k, spots, own, far, frames, out):
    rows = own[0].shape[0]
    counts = [a.shape[1] // 2 for a in own]
    width = sum(counts)
    in_specs = [pl.BlockSpec((rows, count), lambda i, at: (0, i % 2)) for count in counts]
    in_specs += in_specs
    operands = [spots, *own, *far]
    alias = {}
    if out is not None:
        in_specs.append(pl.BlockSpec(memory_space=pl.ANY))
        alias = {len(operands): 0}
        operands.append(out)
    return pl.pallas_call(
        place_kernel,
        grid_spec=pltpu.PrefetchScalarGridSpec(
            num_scalar_prefetch=1,
            grid=(4,),
            in_specs=in_specs,
            out_specs=pl.BlockSpec(
                (rows, width),
                lambda i, at: (0, at[2 + 4 * j + i] * (rows // width) + (k or 0)),
            ),
        ),
        out_shape=jax.ShapeDtypeStruct((rows, frames * rows), F32),
        input_output_aliases=alias,
        compiler_params=pltpu.CompilerParams(vmem_limit_bytes=10 << 20),
        cost_estimate=FREE,
        name="place",
    )(*operands)


def local_pair(library, annulus):
    frames = lax.axis_size("frame")

    def swap_x(a):
        return lax.ppermute(a, "pix", [(0, 1), (1, 0)])

    def swap_y(a):
        return lax.ppermute(a, "frame", [(f, f ^ 2) for f in range(frames)])

    def swap_core(a):
        return lax.ppermute(a, "frame", [(f, f ^ 1) for f in range(frames)])

    def next_z(a):
        return lax.ppermute(a, "frame", [(f, (f + 4) % frames) for f in range(frames)])

    def previous_z(a):
        return lax.ppermute(a, "frame", [((f + 4) % frames, f) for f in range(frames)])

    spots, whole, *chunks = pick(library, annulus)

    other, far = swap_x(whole), swap_y(whole)
    ring = [chunks, cut(next_z(whole), [other, far])]
    ring.append([next_z(a) for a in ring[1]])
    ring.append([previous_z(a) for a in chunks])

    far_other = swap_y(other)
    near = unit_rows(whole, other)
    far = unit_rows(far, far_other)

    keep, chosen, received, paired, columns = {}, {}, {}, {}, {}
    own, sent, back = {}, {}, {}
    last = []

    def send(j, k, *after):
        keep[j, k], chosen[j, k] = choose(j, spots, ring[j][k], ring[j + 2][k], [*last, *after])
        received[j, k] = swap_x(chosen[j, k])
        last[:] = [chosen[j, k]]

    def share(j, k, *after):
        paired[j, k] = pair(keep[j, k], received[j, k], [*last, *after])
        columns[j, k] = [keep[j, k], received[j, k], swap_core(paired[j, k])]
        last[:] = [paired[j, k]]

    def multiply(j, k, *after):
        own[j, k], sent[j, k] = product(k, near, far, columns[j, k], columns[j, 0], [*last, *after])
        back[j, k] = swap_y(sent[j, k])
        last[:] = [sent[j, k]]

    send(0, 0)
    send(0, 1, far_other)
    share(0, 0)
    multiply(0, 0)
    send(0, 2)
    share(0, 1)
    multiply(0, 1)
    send(1, 0)
    share(0, 2, back[0, 0])
    multiply(0, 2)
    send(1, 1)
    share(1, 0, back[0, 1])
    multiply(1, 0)
    send(1, 2)
    share(1, 1, back[0, 2])
    multiply(1, 1)
    share(1, 2, back[1, 0])
    multiply(1, 2)
    n = len(CHUNKS)
    out = place(
        0, None, spots, [own[0, k] for k in range(n)], [back[0, k] for k in range(n)],
        frames // 2, None,
    )
    for k in range(n):
        out = place(1, k, spots, [own[1, k]], [back[1, k]], frames // 2, out)
    return out


def local(library, annulus):
    picked = jnp.take(library, annulus, axis=1)
    total = lax.psum(jnp.sum(picked, axis=1), "pix")
    frame_mean = total / PIX
    centered = picked - frame_mean[:, None]
    squares = lax.psum(jnp.sum(centered * centered, axis=1), "pix")
    unit = centered / jnp.sqrt(squares + EPS)[:, None]
    partial_gram = lax.dot_general(
        unit,
        lax.all_gather(unit, "frame", axis=0, tiled=True),
        (((1,), (1,)), ((), ())),
        precision=lax.Precision.HIGHEST,
        preferred_element_type=jnp.float32,
    )
    return lax.psum_scatter(partial_gram, "pix", scatter_dimension=1, tiled=True)


def solution(mesh):
    placed = (P("frame", "pix"), P("pix"))
    pair = mesh.shape["pix"] == 2 and mesh.shape["frame"] == 16
    return jax.shard_map(
        local_pair if pair else local,
        mesh=mesh, in_specs=placed, out_specs=P("frame", "pix"), check_vma=False,
    )
```

profile of v0, /device:TPU:0, one launch (start us, length us, event | category | flops | bytes accessed | tf_op | source)
XLA Modules:
  0.0 155.6 jit_solution(4949702433427833224)
XLA Ops:
  0.0 1.7 %copy-done = f32[384,1536]{1,0:T(8,128)S(1)} copy-done((f32[384,1536]{1,0:T(8,128)S(1)}, f32[384,1536]{1,0:T(8,128)}, u32[]{:S(2)}) %copy-start) | copy-done | bytes 2359320
  1.7 0.7 copy-done.1
  2.4 2.9 %pick.1 = (s32[10]{0:T(128)S(1)}, f32[392,768]{1,0:T(8,128)S(1)}, f32[136,768]{1,0:T(8,128)S(1)}, f32[128,768]{1,0:T(8,128)S(1)}, f32[128,768]{1,0:T(8,128)S(1)}) custom-call(s32[768]{0:T(1024)S(1)} %copy-done.1, f32[384,1536]{1,0:T(8,128)S(1)} %copy-done), custom_call_target="tpu_custom_call" | custom-call | flops 1 | bytes 1 | tf_op jit(solution)/shard_map/pick/pallas_call | solution.py:76
  5.3 3.0 %collective-permute-start = (f32[392,768]{1,0:T(8,128)S(1)}, f32[392,768]{1,0:T(8,128)S(1)}, u32[]{:S(2)}, u32[]{:S(2)}) collective-permute-start(f32[392,768]{1,0:T(8,128)S(1)} %get-tuple-element.38.a_ref), channel_id=1, source_target_pairs={{0,1},{1,0},{2,3},{3,2},{4,5},{5,4},{6,7},{7,6},{8,9},{9,8},{10,11... | collective-permute-start | bytes 3612680 | tf_op jit(solution)/shard_map/ppermute | solution.py:287
  8.3 1.6 %collective-permute-start.3 = (f32[392,768]{1,0:T(8,128)S(1)}, f32[392,768]{1,0:T(8,128)S(1)}, u32[]{:S(2)}, u32[]{:S(2)}) collective-permute-start(f32[392,768]{1,0:T(8,128)S(1)} %get-tuple-element.38.a_ref), channel_id=1, source_target_pairs={{0,8},{2,10},{4,12},{6,14},{8,16},{10,18},{12,20},{14,22},{16,24},... | collective-permute-start | bytes 3612680 | tf_op jit(solution)/shard_map/ppermute | solution.py:296
  9.9 1.5 collective-permute-start.1
  11.4 23.4 %collective-permute-done.b_ref.refs_0_ = f32[392,768]{1,0:T(8,128)S(1)} collective-permute-done((f32[392,768]{1,0:T(8,128)S(1)}, f32[392,768]{1,0:T(8,128)S(1)}, u32[]{:S(2)}, u32[]{:S(2)}) %collective-permute-start) | collective-permute-done | bytes 1204256 | tf_op jit(solution)/shard_map/ppermute | solution.py:287
  34.8 1.8 %collective-permute-start.2 = (f32[392,768]{1,0:T(8,128)S(1)}, f32[392,768]{1,0:T(8,128)S(1)}, u32[]{:S(2)}, u32[]{:S(2)}) collective-permute-start(f32[392,768]{1,0:T(8,128)S(1)} %collective-permute-done.b_ref.refs_0_), channel_id=1, source_target_pairs={{0,4},{2,6},{4,0},{6,2},{8,12},{10,14},{12,8},{14,10},{16,20},{18,... | collective-permute-start | bytes 3612680 | tf_op jit(solution)/shard_map/ppermute | solution.py:290
  36.6 1.6 collective-permute-done.3.whole_ref
  38.1 0.2 collective-permute-done.1.a_ref.refs_1_
  38.4 0.1 cut.1
  38.4 1.7 %collective-permute-start.7 = (f32[136,768]{1,0:T(8,128)S(1)}, f32[136,768]{1,0:T(8,128)S(1)}, u32[]{:S(2)}, u32[]{:S(2)}) collective-permute-start(f32[136,768]{1,0:T(8,128)S(1)} %get-tuple-element.41.a_ref), channel_id=1, source_target_pairs={{0,8},{2,10},{4,12},{6,14},{8,16},{10,18},{12,20},{14,22},{16,24},... | collective-permute-start | bytes 1253384 | tf_op jit(solution)/shard_map/ppermute | solution.py:296
  40.1 10.2 %collective-permute-done.7.b_ref = f32[136,768]{1,0:T(8,128)S(1)} collective-permute-done((f32[136,768]{1,0:T(8,128)S(1)}, f32[136,768]{1,0:T(8,128)S(1)}, u32[]{:S(2)}, u32[]{:S(2)}) %collective-permute-start.7) | collective-permute-done | bytes 417824 | tf_op jit(solution)/shard_map/ppermute | solution.py:296
  50.3 0.6 choose.6
  51.0 0.8 collective-permute-start.10
  51.8 10.6 %collective-permute-done.6.b_ref = f32[128,768]{1,0:T(8,128)S(1)} collective-permute-done((f32[128,768]{1,0:T(8,128)S(1)}, f32[128,768]{1,0:T(8,128)S(1)}, u32[]{:S(2)}, u32[]{:S(2)}) %collective-permute-start.6) | collective-permute-done | bytes 393248 | tf_op jit(solution)/shard_map/ppermute | solution.py:296
  62.4 1.0 collective-permute-done.2.b_ref.refs_1_
  63.4 0.6 choose.7
  64.0 0.1 collective-permute-start.11
  64.1 1.6 %collective-permute-start.9 = (f32[128,768]{1,0:T(8,128)S(1)}, f32[128,768]{1,0:T(8,128)S(1)}, u32[]{:S(2)}, u32[]{:S(2)}) collective-permute-start(f32[128,768]{1,0:T(8,128)S(1)} %get-tuple-element.39.a_ref), channel_id=1, source_target_pairs={{0,8},{2,10},{4,12},{6,14},{8,16},{10,18},{12,20},{14,22},{16,24},... | collective-permute-start | bytes 1179656 | tf_op jit(solution)/shard_map/ppermute | solution.py:296
  65.7 0.5 collective-permute-start.8
  66.3 0.8 unit_rows.2.refs_0_
  67.1 0.8 unit_rows.3.refs_1_
  67.9 2.2 %product.6 = (f32[384,256]{1,0:T(8,128)S(1)}, f32[384,256]{1,0:T(8,128)S(1)}) custom-call(bf16[768,1536]{1,0:T(8,128)(2,1)S(1)} %unit_rows.2.refs_0_, bf16[768,1536]{1,0:T(8,128)(2,1)S(1)} %unit_rows.3.refs_1_, f32[136,768]{1,0:T(8,128)S(1)} %get-tuple-element.48.a_ref.refs_2_.refs_5_, f32[136,768]{1,0:T(8,128)S(1)} %collective-permute-done.10.b_ref.refs_3_.refs_6_, ...), custom_call_target="tpu_custom_call" | custom-call | flops 1 | bytes 1 | tf_op jit(solution)/shard_map/product/pallas_call | solution.py:229
  70.1 7.3 %collective-permute-done.9.b_ref = f32[128,768]{1,0:T(8,128)S(1)} collective-permute-done((f32[128,768]{1,0:T(8,128)S(1)}, f32[128,768]{1,0:T(8,128)S(1)}, u32[]{:S(2)}, u32[]{:S(2)}) %collective-permute-start.9) | collective-permute-done | bytes 393248 | tf_op jit(solution)/shard_map/ppermute | solution.py:296
  77.4 0.6 choose.8
  78.1 0.1 collective-permute-start.12
  78.2 1.2 collective-permute-start.5
  79.4 1.2 collective-permute-start.15
  80.6 1.5 collective-permute-start.16
  82.1 2.2 %product.7 = (f32[384,256]{1,0:T(8,128)S(1)}, f32[384,256]{1,0:T(8,128)S(1)}) custom-call(bf16[768,1536]{1,0:T(8,128)(2,1)S(1)} %unit_rows.2.refs_0_, bf16[768,1536]{1,0:T(8,128)(2,1)S(1)} %unit_rows.3.refs_1_, f32[128,768]{1,0:T(8,128)S(1)} %get-tuple-element.46.a_ref.refs_2_, f32[128,768]{1,0:T(8,128)S(1)} %collective-permute-done.8.b_ref.refs_3_, ...), custom_call_target="tpu_custom_call" | custom-call | flops 1 | bytes 1 | tf_op jit(solution)/shard_map/product/pallas_call | solution.py:229
  84.3 5.9 %collective-permute-done.5.b_ref = f32[136,768]{1,0:T(8,128)S(1)} collective-permute-done((f32[136,768]{1,0:T(8,128)S(1)}, f32[136,768]{1,0:T(8,128)S(1)}, u32[]{:S(2)}, u32[]{:S(2)}) %collective-permute-start.5) | collective-permute-done | bytes 417824 | tf_op jit(solution)/shard_map/ppermute | solution.py:299
  90.2 0.6 choose.9
  90.8 0.6 collective-permute-done.16.refs_1_.refs_3_
  91.6 0.9 collective-permute-start.13
  92.5 2.7 %collective-permute-start.14 = (f32[128,768]{1,0:T(8,128)S(1)}, f32[128,768]{1,0:T(8,128)S(1)}, u32[]{:S(2)}, u32[]{:S(2)}) collective-permute-start(f32[128,768]{1,0:T(8,128)S(1)} %get-tuple-element.43.a_ref), channel_id=1, source_target_pairs={{8,0},{10,2},{12,4},{14,6},{16,8},{18,10},{20,12},{22,14},{24,16},... | collective-permute-start | bytes 1179656 | tf_op jit(solution)/shard_map/ppermute | solution.py:299
  95.2 1.5 collective-permute-start.18
  96.7 2.2 %product.8 = (f32[384,256]{1,0:T(8,128)S(1)}, f32[384,256]{1,0:T(8,128)S(1)}) custom-call(bf16[768,1536]{1,0:T(8,128)(2,1)S(1)} %unit_rows.2.refs_0_, bf16[768,1536]{1,0:T(8,128)(2,1)S(1)} %unit_rows.3.refs_1_, f32[128,768]{1,0:T(8,128)S(1)} %get-tuple-element.54.a_ref.refs_2_, f32[128,768]{1,0:T(8,128)S(1)} %collective-permute-done.15.b_ref.refs_3_, ...), custom_call_target="tpu_custom_call" | custom-call | flops 1 | bytes 1 | tf_op jit(solution)/shard_map/product/pallas_call | solution.py:229
  99.0 4.9 %collective-permute-done.14.b_ref = f32[128,768]{1,0:T(8,128)S(1)} collective-permute-done((f32[128,768]{1,0:T(8,128)S(1)}, f32[128,768]{1,0:T(8,128)S(1)}, u32[]{:S(2)}, u32[]{:S(2)}) %collective-permute-start.14) | collective-permute-done | bytes 393248 | tf_op jit(solution)/shard_map/ppermute | solution.py:299
  103.9 0.6 choose.10
  104.5 1.6 %collective-permute-done.18.refs_1_.refs_4_ = f32[384,256]{1,0:T(8,128)S(1)} collective-permute-done((f32[384,256]{1,0:T(8,128)S(1)}, f32[384,256]{1,0:T(8,128)S(1)}, u32[]{:S(2)}, u32[]{:S(2)}) %collective-permute-start.18) | collective-permute-done | bytes 393248 | tf_op jit(solution)/shard_map/ppermute | solution.py:290
  106.3 2.9 %collective-permute-start.4 = (f32[128,768]{1,0:T(8,128)S(1)}, f32[128,768]{1,0:T(8,128)S(1)}, u32[]{:S(2)}, u32[]{:S(2)}) collective-permute-start(f32[128,768]{1,0:T(8,128)S(1)} %get-tuple-element.40.a_ref), channel_id=1, source_target_pairs={{8,0},{10,2},{12,4},{14,6},{16,8},{18,10},{20,12},{22,14},{24,16},... | collective-permute-start | bytes 1179656 | tf_op jit(solution)/shard_map/ppermute | solution.py:299
  109.2 0.8 collective-permute-start.21
  110.0 1.5 collective-permute-start.22
  111.5 2.2 %product.9 = (f32[384,256]{1,0:T(8,128)S(1)}, f32[384,256]{1,0:T(8,128)S(1)}) custom-call(bf16[768,1536]{1,0:T(8,128)(2,1)S(1)} %unit_rows.2.refs_0_, bf16[768,1536]{1,0:T(8,128)(2,1)S(1)} %unit_rows.3.refs_1_, f32[136,768]{1,0:T(8,128)S(1)} %get-tuple-element.52.a_ref.refs_2_.refs_5_, f32[136,768]{1,0:T(8,128)S(1)} %collective-permute-done.13.b_ref.refs_3_.refs_6_, ...), custom_call_target="tpu_custom_call" | custom-call | flops 1 | bytes 1 | tf_op jit(solution)/shard_map/product/pallas_call | solution.py:229
  113.8 4.2 %collective-permute-done.4.b_ref = f32[128,768]{1,0:T(8,128)S(1)} collective-permute-done((f32[128,768]{1,0:T(8,128)S(1)}, f32[128,768]{1,0:T(8,128)S(1)}, u32[]{:S(2)}, u32[]{:S(2)}) %collective-permute-start.4) | collective-permute-done | bytes 393248 | tf_op jit(solution)/shard_map/ppermute | solution.py:299
  118.0 0.6 choose.11
  118.6 1.6 %collective-permute-done.21.b_ref.refs_3_ = f32[128,768]{1,0:T(8,128)S(1)} collective-permute-done((f32[128,768]{1,0:T(8,128)S(1)}, f32[128,768]{1,0:T(8,128)S(1)}, u32[]{:S(2)}, u32[]{:S(2)}) %collective-permute-start.21) | collective-permute-done | bytes 393248 | tf_op jit(solution)/shard_map/ppermute | solution.py:287
  120.2 0.5 collective-permute-done.22.refs_1_.refs_5_
  120.9 1.3 collective-permute-start.20
  122.1 1.5 collective-permute-start.24
  123.7 2.2 %product.10 = (f32[384,256]{1,0:T(8,128)S(1)}, f32[384,256]{1,0:T(8,128)S(1)}) custom-call(bf16[768,1536]{1,0:T(8,128)(2,1)S(1)} %unit_rows.2.refs_0_, bf16[768,1536]{1,0:T(8,128)(2,1)S(1)} %unit_rows.3.refs_1_, f32[128,768]{1,0:T(8,128)S(1)} %get-tuple-element.60.a_ref.refs_2_, f32[128,768]{1,0:T(8,128)S(1)} %collective-permute-done.21.b_ref.refs_3_, ...), custom_call_target="tpu_custom_call" | custom-call | flops 1 | bytes 1 | tf_op jit(solution)/shard_map/product/pallas_call | solution.py:229
  125.9 6.5 %collective-permute-done.20.b_ref.refs_3_ = f32[128,768]{1,0:T(8,128)S(1)} collective-permute-done((f32[128,768]{1,0:T(8,128)S(1)}, f32[128,768]{1,0:T(8,128)S(1)}, u32[]{:S(2)}, u32[]{:S(2)}) %collective-permute-start.20) | collective-permute-done | bytes 393248 | tf_op jit(solution)/shard_map/ppermute | solution.py:287
  132.4 0.9 collective-permute-done.24.refs_1_
  133.5 1.6 %collective-permute-start.27 = (f32[384,256]{1,0:T(8,128)S(1)}, f32[384,256]{1,0:T(8,128)S(1)}, u32[]{:S(2)}, u32[]{:S(2)}) collective-permute-start(f32[384,256]{1,0:T(8,128)S(1)} %get-tuple-element.61.refs_0_), channel_id=1, source_target_pairs={{0,4},{2,6},{4,0},{6,2},{8,12},{10,14},{12,8},{14,10},{16,20},{18,... | collective-permute-start | bytes 1179656 | tf_op jit(solution)/shard_map/ppermute | solution.py:290
  135.1 0.7 collective-permute-done.25.refs_4_
  135.7 2.2 %product.11 = (f32[384,256]{1,0:T(8,128)S(1)}, f32[384,256]{1,0:T(8,128)S(1)}) custom-call(bf16[768,1536]{1,0:T(8,128)(2,1)S(1)} %unit_rows.2.refs_0_, bf16[768,1536]{1,0:T(8,128)(2,1)S(1)} %unit_rows.3.refs_1_, f32[128,768]{1,0:T(8,128)S(1)} %get-tuple-element.58.a_ref.refs_2_, f32[128,768]{1,0:T(8,128)S(1)} %collective-permute-done.20.b_ref.refs_3_, ...), custom_call_target="tpu_custom_call" | custom-call | flops 1 | bytes 1 | tf_op jit(solution)/shard_map/product/pallas_call | solution.py:229
  138.0 1.6 %collective-permute-start.26 = (f32[384,256]{1,0:T(8,128)S(1)}, f32[384,256]{1,0:T(8,128)S(1)}, u32[]{:S(2)}, u32[]{:S(2)}) collective-permute-start(f32[384,256]{1,0:T(8,128)S(1)} %get-tuple-element.63), channel_id=1, source_target_pairs={{0,4},{2,6},{4,0},{6,2},{8,12},{10,14},{12,8},{14,10},{16,20},{18,... | collective-permute-start | bytes 1179656 | tf_op jit(solution)/shard_map/ppermute | solution.py:290
  139.6 2.8 %place.4.refs_2_ = f32[384,3072]{1,0:T(8,128)} custom-call(s32[10]{0:T(128)S(1)} %get-tuple-element.37.first_ref.at_ref, f32[384,256]{1,0:T(8,128)S(1)} %get-tuple-element.66.refs_0_, f32[384,256]{1,0:T(8,128)S(1)} %get-tuple-element.67.refs_1_, f32[384,256]{1,0:T(8,128)S(1)} %get-tuple-element.68.refs_2_, ...), custom_call_target="tpu_custom_call" | custom-call | flops 1 | bytes 1 | tf_op jit(solution)/shard_map/place/pallas_call | solution.py:264
  142.4 2.1 %place.5.refs_2_ = f32[384,3072]{1,0:T(8,128)} custom-call(s32[10]{0:T(128)S(1)} %get-tuple-element.37.first_ref.at_ref, f32[384,256]{1,0:T(8,128)S(1)} %get-tuple-element.65.refs_0_, f32[384,256]{1,0:T(8,128)S(1)} %collective-permute-done.24.refs_1_, f32[384,3072]{1,0:T(8,128)} %place.4.refs_2_), custom_call_target="tpu_custom_call", output_to_operand_aliasing={{}: (3, {})} | custom-call | flops 1 | bytes 1 | tf_op jit(solution)/shard_map/place/pallas_call | solution.py:264
  144.5 0.9 collective-permute-done.27.refs_1_
  145.5 2.2 %place.6.refs_2_ = f32[384,3072]{1,0:T(8,128)} custom-call(s32[10]{0:T(128)S(1)} %get-tuple-element.37.first_ref.at_ref, f32[384,256]{1,0:T(8,128)S(1)} %get-tuple-element.64.refs_0_, f32[384,256]{1,0:T(8,128)S(1)} %collective-permute-done.27.refs_1_, f32[384,3072]{1,0:T(8,128)} %place.5.refs_2_), custom_call_target="tpu_custom_call", output_to_operand_aliasing={{}: (3, {})} | custom-call | flops 1 | bytes 1 | tf_op jit(solution)/shard_map/place/pallas_call | solution.py:264
  147.6 5.8 %collective-permute-done.26.refs_1_ = f32[384,256]{1,0:T(8,128)S(1)} collective-permute-done((f32[384,256]{1,0:T(8,128)S(1)}, f32[384,256]{1,0:T(8,128)S(1)}, u32[]{:S(2)}, u32[]{:S(2)}) %collective-permute-start.26) | collective-permute-done | bytes 393248 | tf_op jit(solution)/shard_map/ppermute | solution.py:290
  153.4 2.2 %place.7 = f32[384,3072]{1,0:T(8,128)} custom-call(s32[10]{0:T(128)S(1)} %get-tuple-element.37.first_ref.at_ref, f32[384,256]{1,0:T(8,128)S(1)} %get-tuple-element.62.refs_0_, f32[384,256]{1,0:T(8,128)S(1)} %collective-permute-done.26.refs_1_, f32[384,3072]{1,0:T(8,128)} %place.6.refs_2_), custom_call_target="tpu_custom_call", output_to_operand_aliasing={{}: (3, {})} | custom-call | flops 1 | bytes 1 | tf_op jit(solution)/shard_map/place/pallas_call | solution.py:264
  (22 shorter events, 0.6 us)
Async XLA Ops:
  0.0 1.7 %copy-start = (f32[384,1536]{1,0:T(8,128)S(1)}, f32[384,1536]{1,0:T(8,128)}, u32[]{:S(2)}) copy-start(f32[384,1536]{1,0:T(8,128)} %library_ref.1) | copy-start | bytes 7077892
  1.7 0.7 copy-start.1
  5.3 29.5 %collective-permute-start = (f32[392,768]{1,0:T(8,128)S(1)}, f32[392,768]{1,0:T(8,128)S(1)}, u32[]{:S(2)}, u32[]{:S(2)}) collective-permute-start(f32[392,768]{1,0:T(8,128)S(1)} %get-tuple-element.38.a_ref), channel_id=1, source_target_pairs={{0,1},{1,0},{2,3},{3,2},{4,5},{5,4},{6,7},{7,6},{8,9},{9,8},{10,11... | collective-permute-start | bytes 3612680 | tf_op jit(solution)/shard_map/ppermute | solution.py:287
  8.3 29.8 %collective-permute-start.3 = (f32[392,768]{1,0:T(8,128)S(1)}, f32[392,768]{1,0:T(8,128)S(1)}, u32[]{:S(2)}, u32[]{:S(2)}) collective-permute-start(f32[392,768]{1,0:T(8,128)S(1)} %get-tuple-element.38.a_ref), channel_id=1, source_target_pairs={{0,8},{2,10},{4,12},{6,14},{8,16},{10,18},{12,20},{14,22},{16,24},... | collective-permute-start | bytes 3612680 | tf_op jit(solution)/shard_map/ppermute | solution.py:296
  9.9 28.5 %collective-permute-start.1 = (f32[392,768]{1,0:T(8,128)S(1)}, f32[392,768]{1,0:T(8,128)S(1)}, u32[]{:S(2)}, u32[]{:S(2)}) collective-permute-start(f32[392,768]{1,0:T(8,128)S(1)} %get-tuple-element.38.a_ref), channel_id=1, source_target_pairs={{0,4},{2,6},{4,0},{6,2},{8,12},{10,14},{12,8},{14,10},{16,20},{18,... | collective-permute-start | bytes 3612680 | tf_op jit(solution)/shard_map/ppermute | solution.py:290
  34.8 28.6 %collective-permute-start.2 = (f32[392,768]{1,0:T(8,128)S(1)}, f32[392,768]{1,0:T(8,128)S(1)}, u32[]{:S(2)}, u32[]{:S(2)}) collective-permute-start(f32[392,768]{1,0:T(8,128)S(1)} %collective-permute-done.b_ref.refs_0_), channel_id=1, source_target_pairs={{0,4},{2,6},{4,0},{6,2},{8,12},{10,14},{12,8},{14,10},{16,20},{18,... | collective-permute-start | bytes 3612680 | tf_op jit(solution)/shard_map/ppermute | solution.py:290
  38.4 11.9 %collective-permute-start.7 = (f32[136,768]{1,0:T(8,128)S(1)}, f32[136,768]{1,0:T(8,128)S(1)}, u32[]{:S(2)}, u32[]{:S(2)}) collective-permute-start(f32[136,768]{1,0:T(8,128)S(1)} %get-tuple-element.41.a_ref), channel_id=1, source_target_pairs={{0,8},{2,10},{4,12},{6,14},{8,16},{10,18},{12,20},{14,22},{16,24},... | collective-permute-start | bytes 1253384 | tf_op jit(solution)/shard_map/ppermute | solution.py:296
  51.0 13.0 %collective-permute-start.10 = (f32[136,768]{1,0:T(8,128)S(1)}, f32[136,768]{1,0:T(8,128)S(1)}, u32[]{:S(2)}, u32[]{:S(2)}) collective-permute-start(f32[136,768]{1,0:T(8,128)S(1)} %get-tuple-element.45.refs_0_), channel_id=1, source_target_pairs={{0,1},{1,0},{2,3},{3,2},{4,5},{5,4},{6,7},{7,6},{8,9},{9,8},{10,11... | collective-permute-start | bytes 1253384 | tf_op jit(solution)/shard_map/ppermute | solution.py:287
  51.8 10.6 %collective-permute-start.6 = (f32[128,768]{1,0:T(8,128)S(1)}, f32[128,768]{1,0:T(8,128)S(1)}, u32[]{:S(2)}, u32[]{:S(2)}) collective-permute-start(f32[128,768]{1,0:T(8,128)S(1)} %get-tuple-element.44.a_ref), channel_id=1, source_target_pairs={{0,8},{2,10},{4,12},{6,14},{8,16},{10,18},{12,20},{14,22},{16,24},... | collective-permute-start | bytes 1179656 | tf_op jit(solution)/shard_map/ppermute | solution.py:296
  64.0 3.8 %collective-permute-start.11 = (f32[2,136,768]{2,1,0:T(8,128)S(1)}, f32[2,136,768]{2,1,0:T(8,128)S(1)}, u32[]{:S(2)}, u32[]{:S(2)}) collective-permute-start(f32[2,136,768]{2,1,0:T(8,128)S(1)} %pair.6.refs_5_), channel_id=1, source_target_pairs={{0,2},{2,0},{4,6},{6,4},{8,10},{10,8},{12,14},{14,12},{16,18},{18,... | collective-permute-start | bytes 2506760 | tf_op jit(solution)/shard_map/ppermute | solution.py:293
  64.1 13.3 %collective-permute-start.9 = (f32[128,768]{1,0:T(8,128)S(1)}, f32[128,768]{1,0:T(8,128)S(1)}, u32[]{:S(2)}, u32[]{:S(2)}) collective-permute-start(f32[128,768]{1,0:T(8,128)S(1)} %get-tuple-element.39.a_ref), channel_id=1, source_target_pairs={{0,8},{2,10},{4,12},{6,14},{8,16},{10,18},{12,20},{14,22},{16,24},... | collective-permute-start | bytes 1179656 | tf_op jit(solution)/shard_map/ppermute | solution.py:296
  65.7 12.3 %collective-permute-start.8 = (f32[128,768]{1,0:T(8,128)S(1)}, f32[128,768]{1,0:T(8,128)S(1)}, u32[]{:S(2)}, u32[]{:S(2)}) collective-permute-start(f32[128,768]{1,0:T(8,128)S(1)} %get-tuple-element.47.refs_0_), channel_id=1, source_target_pairs={{0,1},{1,0},{2,3},{3,2},{4,5},{5,4},{6,7},{7,6},{8,9},{9,8},{10,11... | collective-permute-start | bytes 1179656 | tf_op jit(solution)/shard_map/ppermute | solution.py:287
  78.1 4.0 %collective-permute-start.12 = (f32[2,128,768]{2,1,0:T(8,128)S(1)}, f32[2,128,768]{2,1,0:T(8,128)S(1)}, u32[]{:S(2)}, u32[]{:S(2)}) collective-permute-start(f32[2,128,768]{2,1,0:T(8,128)S(1)} %pair.7.refs_8_), channel_id=1, source_target_pairs={{0,2},{2,0},{4,6},{6,4},{8,10},{10,8},{12,14},{14,12},{16,18},{18,... | collective-permute-start | bytes 2359304 | tf_op jit(solution)/shard_map/ppermute | solution.py:293
  78.2 12.0 %collective-permute-start.5 = (f32[136,768]{1,0:T(8,128)S(1)}, f32[136,768]{1,0:T(8,128)S(1)}, u32[]{:S(2)}, u32[]{:S(2)}) collective-permute-start(f32[136,768]{1,0:T(8,128)S(1)} %get-tuple-element.42.a_ref), channel_id=1, source_target_pairs={{8,0},{10,2},{12,4},{14,6},{16,8},{18,10},{20,12},{22,14},{24,16},... | collective-permute-start | bytes 1253384 | tf_op jit(solution)/shard_map/ppermute | solution.py:299
  79.4 11.5 %collective-permute-start.15 = (f32[128,768]{1,0:T(8,128)S(1)}, f32[128,768]{1,0:T(8,128)S(1)}, u32[]{:S(2)}, u32[]{:S(2)}) collective-permute-start(f32[128,768]{1,0:T(8,128)S(1)} %get-tuple-element.50.refs_0_), channel_id=1, source_target_pairs={{0,1},{1,0},{2,3},{3,2},{4,5},{5,4},{6,7},{7,6},{8,9},{9,8},{10,11... | collective-permute-start | bytes 1179656 | tf_op jit(solution)/shard_map/ppermute | solution.py:287
  80.6 10.9 %collective-permute-start.16 = (f32[384,256]{1,0:T(8,128)S(1)}, f32[384,256]{1,0:T(8,128)S(1)}, u32[]{:S(2)}, u32[]{:S(2)}) collective-permute-start(f32[384,256]{1,0:T(8,128)S(1)} %get-tuple-element.49.refs_0_), channel_id=1, source_target_pairs={{0,4},{2,6},{4,0},{6,2},{8,12},{10,14},{12,8},{14,10},{16,20},{18,... | collective-permute-start | bytes 1179656 | tf_op jit(solution)/shard_map/ppermute | solution.py:290
  91.5 5.2 %collective-permute-start.17 = (f32[2,128,768]{2,1,0:T(8,128)S(1)}, f32[2,128,768]{2,1,0:T(8,128)S(1)}, u32[]{:S(2)}, u32[]{:S(2)}) collective-permute-start(f32[2,128,768]{2,1,0:T(8,128)S(1)} %pair.8.refs_8_), channel_id=1, source_target_pairs={{0,2},{2,0},{4,6},{6,4},{8,10},{10,8},{12,14},{14,12},{16,18},{18,... | collective-permute-start | bytes 2359304 | tf_op jit(solution)/shard_map/ppermute | solution.py:293
  91.6 14.5 %collective-permute-start.13 = (f32[136,768]{1,0:T(8,128)S(1)}, f32[136,768]{1,0:T(8,128)S(1)}, u32[]{:S(2)}, u32[]{:S(2)}) collective-permute-start(f32[136,768]{1,0:T(8,128)S(1)} %get-tuple-element.53.refs_0_), channel_id=1, source_target_pairs={{0,1},{1,0},{2,3},{3,2},{4,5},{5,4},{6,7},{7,6},{8,9},{9,8},{10,11... | collective-permute-start | bytes 1253384 | tf_op jit(solution)/shard_map/ppermute | solution.py:287
  92.5 11.4 %collective-permute-start.14 = (f32[128,768]{1,0:T(8,128)S(1)}, f32[128,768]{1,0:T(8,128)S(1)}, u32[]{:S(2)}, u32[]{:S(2)}) collective-permute-start(f32[128,768]{1,0:T(8,128)S(1)} %get-tuple-element.43.a_ref), channel_id=1, source_target_pairs={{8,0},{10,2},{12,4},{14,6},{16,8},{18,10},{20,12},{22,14},{24,16},... | collective-permute-start | bytes 1179656 | tf_op jit(solution)/shard_map/ppermute | solution.py:299
  95.2 10.9 %collective-permute-start.18 = (f32[384,256]{1,0:T(8,128)S(1)}, f32[384,256]{1,0:T(8,128)S(1)}, u32[]{:S(2)}, u32[]{:S(2)}) collective-permute-start(f32[384,256]{1,0:T(8,128)S(1)} %get-tuple-element.51.refs_0_), channel_id=1, source_target_pairs={{0,4},{2,6},{4,0},{6,2},{8,12},{10,14},{12,8},{14,10},{16,20},{18,... | collective-permute-start | bytes 1179656 | tf_op jit(solution)/shard_map/ppermute | solution.py:290
  106.2 5.3 %collective-permute-start.19 = (f32[2,136,768]{2,1,0:T(8,128)S(1)}, f32[2,136,768]{2,1,0:T(8,128)S(1)}, u32[]{:S(2)}, u32[]{:S(2)}) collective-permute-start(f32[2,136,768]{2,1,0:T(8,128)S(1)} %pair.9.refs_5_), channel_id=1, source_target_pairs={{0,2},{2,0},{4,6},{6,4},{8,10},{10,8},{12,14},{14,12},{16,18},{18,... | collective-permute-start | bytes 2506760 | tf_op jit(solution)/shard_map/ppermute | solution.py:293
  106.3 11.7 %collective-permute-start.4 = (f32[128,768]{1,0:T(8,128)S(1)}, f32[128,768]{1,0:T(8,128)S(1)}, u32[]{:S(2)}, u32[]{:S(2)}) collective-permute-start(f32[128,768]{1,0:T(8,128)S(1)} %get-tuple-element.40.a_ref), channel_id=1, source_target_pairs={{8,0},{10,2},{12,4},{14,6},{16,8},{18,10},{20,12},{22,14},{24,16},... | collective-permute-start | bytes 1179656 | tf_op jit(solution)/shard_map/ppermute | solution.py:299
  109.2 11.0 %collective-permute-start.21 = (f32[128,768]{1,0:T(8,128)S(1)}, f32[128,768]{1,0:T(8,128)S(1)}, u32[]{:S(2)}, u32[]{:S(2)}) collective-permute-start(f32[128,768]{1,0:T(8,128)S(1)} %get-tuple-element.56.refs_0_), channel_id=1, source_target_pairs={{0,1},{1,0},{2,3},{3,2},{4,5},{5,4},{6,7},{7,6},{8,9},{9,8},{10,11... | collective-permute-start | bytes 1179656 | tf_op jit(solution)/shard_map/ppermute | solution.py:287
  110.0 10.7 %collective-permute-start.22 = (f32[384,256]{1,0:T(8,128)S(1)}, f32[384,256]{1,0:T(8,128)S(1)}, u32[]{:S(2)}, u32[]{:S(2)}) collective-permute-start(f32[384,256]{1,0:T(8,128)S(1)} %get-tuple-element.55.refs_0_), channel_id=1, source_target_pairs={{0,4},{2,6},{4,0},{6,2},{8,12},{10,14},{12,8},{14,10},{16,20},{18,... | collective-permute-start | bytes 1179656 | tf_op jit(solution)/shard_map/ppermute | solution.py:290
  120.8 2.9 %collective-permute-start.23 = (f32[2,128,768]{2,1,0:T(8,128)S(1)}, f32[2,128,768]{2,1,0:T(8,128)S(1)}, u32[]{:S(2)}, u32[]{:S(2)}) collective-permute-start(f32[2,128,768]{2,1,0:T(8,128)S(1)} %pair.10.refs_8_), channel_id=1, source_target_pairs={{0,2},{2,0},{4,6},{6,4},{8,10},{10,8},{12,14},{14,12},{16,18},{18,... | collective-permute-start | bytes 2359304 | tf_op jit(solution)/shard_map/ppermute | solution.py:293
  120.9 11.5 %collective-permute-start.20 = (f32[128,768]{1,0:T(8,128)S(1)}, f32[128,768]{1,0:T(8,128)S(1)}, u32[]{:S(2)}, u32[]{:S(2)}) collective-permute-start(f32[128,768]{1,0:T(8,128)S(1)} %get-tuple-element.59.refs_0_), channel_id=1, source_target_pairs={{0,1},{1,0},{2,3},{3,2},{4,5},{5,4},{6,7},{7,6},{8,9},{9,8},{10,11... | collective-permute-start | bytes 1179656 | tf_op jit(solution)/shard_map/ppermute | solution.py:287
  122.1 11.2 %collective-permute-start.24 = (f32[384,256]{1,0:T(8,128)S(1)}, f32[384,256]{1,0:T(8,128)S(1)}, u32[]{:S(2)}, u32[]{:S(2)}) collective-permute-start(f32[384,256]{1,0:T(8,128)S(1)} %get-tuple-element.57.refs_0_), channel_id=1, source_target_pairs={{0,4},{2,6},{4,0},{6,2},{8,12},{10,14},{12,8},{14,10},{16,20},{18,... | collective-permute-start | bytes 1179656 | tf_op jit(solution)/shard_map/ppermute | solution.py:290
  133.4 2.4 %collective-permute-start.25 = (f32[2,128,768]{2,1,0:T(8,128)S(1)}, f32[2,128,768]{2,1,0:T(8,128)S(1)}, u32[]{:S(2)}, u32[]{:S(2)}) collective-permute-start(f32[2,128,768]{2,1,0:T(8,128)S(1)} %pair.11.refs_8_), channel_id=1, source_target_pairs={{0,2},{2,0},{4,6},{6,4},{8,10},{10,8},{12,14},{14,12},{16,18},{18,... | collective-permute-start | bytes 2359304 | tf_op jit(solution)/shard_map/ppermute | solution.py:293
  133.5 12.0 %collective-permute-start.27 = (f32[384,256]{1,0:T(8,128)S(1)}, f32[384,256]{1,0:T(8,128)S(1)}, u32[]{:S(2)}, u32[]{:S(2)}) collective-permute-start(f32[384,256]{1,0:T(8,128)S(1)} %get-tuple-element.61.refs_0_), channel_id=1, source_target_pairs={{0,4},{2,6},{4,0},{6,2},{8,12},{10,14},{12,8},{14,10},{16,20},{18,... | collective-permute-start | bytes 1179656 | tf_op jit(solution)/shard_map/ppermute | solution.py:290
  138.0 15.4 %collective-permute-start.26 = (f32[384,256]{1,0:T(8,128)S(1)}, f32[384,256]{1,0:T(8,128)S(1)}, u32[]{:S(2)}, u32[]{:S(2)}) collective-permute-start(f32[384,256]{1,0:T(8,128)S(1)} %get-tuple-element.63), channel_id=1, source_target_pairs={{0,4},{2,6},{4,0},{6,2},{8,12},{10,14},{12,8},{14,10},{16,20},{18,... | collective-permute-start | bytes 1179656 | tf_op jit(solution)/shard_map/ppermute | solution.py:290
where the time goes:
time: 156 us
  waiting for transfers between devices  88.6 us (57%)
  starting transfers between devices  33.3 us (21%)
  Pallas kernels  31.1 us (20%)
  local copies, waits for them, and re-layouts  2.35 us (2%)
    ppermute x7, waiting for transfers between devices, swap_x(): return lax.ppermute(a, 'pix', [(0, 1), (1, 0)])  31.5 us
    ppermute x4, waiting for transfers between devices, next_z(): lax.ppermute(a, 'frame', [(f, (f + 4) % frames) for f in range(frames)])  29.6 us
    ppermute x3, waiting for transfers between devices, previous_z(): lax.ppermute(a, 'frame', [((f + 4) % frames, f) for f in range(frames)])  15.1 us
    pallas_call x6, Pallas kernels, product(): pl.pallas_call(functools.partial(product_kernel, start, count), grid=(1,)...  13.4 us
    ppermute x8, starting transfers between devices, swap_y(): return lax.ppermute(a, 'frame', [(f, f ^ 2) for f in range(frames)])  12.5 us
    ppermute x8, waiting for transfers between devices, swap_y(): return lax.ppermute(a, 'frame', [(f, f ^ 2) for f in range(frames)])  11.7 us
    pallas_call x4, Pallas kernels, place(): pl.pallas_call(place_kernel, grid_spec=pltpu.PrefetchScalarGridSpec(num_s...  9.24 us
    ppermute x7, starting transfers between devices, swap_x(): return lax.ppermute(a, 'pix', [(0, 1), (1, 0)])  8.56 us
  transfers between devices with their start and end apart: 28, of which 19 were waited for; matrix products, arithmetic and copies ran while one was open for 0% of the time, Pallas kernels for 17%

commit v1 on v0

--- a/solution.py
+++ b/solution.py
@@ -301,9 +301,9 @@
     spots, whole, *chunks = pick(library, annulus)
 
     other, far = swap_x(whole), swap_y(whole)
-    ring = [chunks, cut(next_z(whole), [other, far])]
-    ring.append([next_z(a) for a in ring[1]])
-    ring.append([previous_z(a) for a in chunks])
+    back_z = [previous_z(a) for a in chunks]
+    ring = [chunks, cut(next_z(whole), [other, far, back_z[0]])]
+    ring += [[next_z(a) for a in ring[1]], back_z]
 
     far_other = swap_y(other)
     near = unit_rows(whole, other)
@@ -311,48 +311,44 @@
 
     keep, chosen, received, paired, columns = {}, {}, {}, {}, {}
     own, sent, back = {}, {}, {}
-    last = []
 
     def send(j, k, *after):
-        keep[j, k], chosen[j, k] = choose(j, spots, ring[j][k], ring[j + 2][k], [*last, *after])
+        keep[j, k], chosen[j, k] = choose(1 - j, spots, ring[1 - j][k], ring[3 - j][k], after)
         received[j, k] = swap_x(chosen[j, k])
-        last[:] = [chosen[j, k]]
 
     def share(j, k, *after):
-        paired[j, k] = pair(keep[j, k], received[j, k], [*last, *after])
+        paired[j, k] = pair(keep[j, k], received[j, k], after)
         columns[j, k] = [keep[j, k], received[j, k], swap_core(paired[j, k])]
-        last[:] = [paired[j, k]]
 
     def multiply(j, k, *after):
-        own[j, k], sent[j, k] = product(k, near, far, columns[j, k], columns[j, 0], [*last, *after])
+        own[j, k], sent[j, k] = product(k, near, far, columns[j, k], columns[j, 0], after)
         back[j, k] = swap_y(sent[j, k])
-        last[:] = [sent[j, k]]
 
     send(0, 0)
-    send(0, 1, far_other)
+    send(0, 1)
     share(0, 0)
     multiply(0, 0)
+    share(0, 1)
     send(0, 2)
-    share(0, 1)
     multiply(0, 1)
+    share(0, 2, sent[0, 0], far_other)
+    multiply(0, 2)
     send(1, 0)
-    share(0, 2, back[0, 0])
-    multiply(0, 2)
-    send(1, 1)
-    share(1, 0, back[0, 1])
+    send(1, 1, sent[0, 1], back[0, 0], sent[0, 2])
+    send(1, 2, sent[0, 2])
+    share(1, 0, back[0, 0])
     multiply(1, 0)
-    send(1, 2)
-    share(1, 1, back[0, 2])
-    multiply(1, 1)
-    share(1, 2, back[1, 0])
+    share(1, 1, back[0, 1])
+    multiply(1, 1, sent[0, 0])
+    share(1, 2, back[0, 2])
     multiply(1, 2)
     n = len(CHUNKS)
     out = place(
-        0, None, spots, [own[0, k] for k in range(n)], [back[0, k] for k in range(n)],
+        1, None, spots, [own[0, k] for k in range(n)], [back[0, k] for k in range(n)],
         frames // 2, None,
     )
     for k in range(n):
-        out = place(1, k, spots, [own[1, k]], [back[1, k]], frames // 2, out)
+        out = place(0, k, spots, [own[1, k]], [back[1, k]], frames // 2, out)
     return out
 
 

time: 156 us -> 149 us (0.955)
  waiting for transfers between devices: 88.6 us -> 84.8 us
  starting transfers between devices: 33.3 us -> 30 us
    ppermute x3, waiting for transfers between devices: 15.1 us -> 41.8 us  [previous_z(): lax.ppermute(a, 'frame', [((f + 4) % frames, f) for f in range(frames)])]
    ppermute x4, waiting for transfers between devices: 29.6 us -> 10.1 us  [next_z(): lax.ppermute(a, 'frame', [(f, (f + 4) % frames) for f in range(frames)])]
    ppermute x7, waiting for transfers between devices: 31.5 us -> 16.1 us  [swap_x(): return lax.ppermute(a, 'pix', [(0, 1), (1, 0)])]
    ppermute x8, waiting for transfers between devices: 11.7 us -> 16.9 us  [swap_y(): return lax.ppermute(a, 'frame', [(f, f ^ 2) for f in range(frames)])]
    ppermute x3, starting transfers between devices: 6.83 us -> 4.67 us  [previous_z(): lax.ppermute(a, 'frame', [((f + 4) % frames, f) for f in range(frames)])]
  transfers between devices with their start and end apart: 28 -> 28, of which waited for: 19 -> 14; matrix products, arithmetic and copies ran while one was open for 0% -> 0% of each run, Pallas kernels for 17% -> 17%
where the time goes in v1:
time: 149 us
  waiting for transfers between devices  84.8 us (57%)
  Pallas kernels  31.1 us (21%)
  starting transfers between devices  30 us (20%)
  local copies, waits for them, and re-layouts  2.35 us (2%)
    ppermute x3, waiting for transfers between devices, previous_z(): lax.ppermute(a, 'frame', [((f + 4) % frames, f) for f in range(frames)])  41.8 us
    ppermute x8, waiting for transfers between devices, swap_y(): return lax.ppermute(a, 'frame', [(f, f ^ 2) for f in range(frames)])  16.9 us
    ppermute x7, waiting for transfers between devices, swap_x(): return lax.ppermute(a, 'pix', [(0, 1), (1, 0)])  16.1 us
    pallas_call x6, Pallas kernels, product(): pl.pallas_call(functools.partial(product_kernel, start, count), grid=(1,)...  13.4 us
    ppermute x8, starting transfers between devices, swap_y(): return lax.ppermute(a, 'frame', [(f, f ^ 2) for f in range(frames)])  11 us
    ppermute x4, waiting for transfers between devices, next_z(): lax.ppermute(a, 'frame', [(f, (f + 4) % frames) for f in range(frames)])  10.1 us
    pallas_call x4, Pallas kernels, place(): pl.pallas_call(place_kernel, grid_spec=pltpu.PrefetchScalarGridSpec(num_s...  9.24 us
    ppermute x7, starting transfers between devices, swap_x(): return lax.ppermute(a, 'pix', [(0, 1), (1, 0)])  9.1 us
  transfers between devices with their start and end apart: 28, of which 14 were waited for; matrix products, arithmetic and copies ran while one was open for 0% of the time, Pallas kernels for 17%

profile of v1, /device:TPU:0, one launch (start us, length us, event | category | flops | bytes accessed | tf_op | source)
XLA Modules:
  0.0 148.6 jit_solution(12699326855490162158)
XLA Ops:
  0.0 1.7 %copy-done = f32[384,1536]{1,0:T(8,128)S(1)} copy-done((f32[384,1536]{1,0:T(8,128)S(1)}, f32[384,1536]{1,0:T(8,128)}, u32[]{:S(2)}) %copy-start) | copy-done | bytes 2359320
  1.7 0.7 copy-done.1
  2.4 2.9 %pick.1 = (s32[10]{0:T(128)S(1)}, f32[392,768]{1,0:T(8,128)S(1)}, f32[136,768]{1,0:T(8,128)S(1)}, f32[128,768]{1,0:T(8,128)S(1)}, f32[128,768]{1,0:T(8,128)S(1)}) custom-call(s32[768]{0:T(1024)S(1)} %copy-done.1, f32[384,1536]{1,0:T(8,128)S(1)} %copy-done), custom_call_target="tpu_custom_call" | custom-call | flops 1 | bytes 1 | tf_op jit(solution)/shard_map/pick/pallas_call | solution.py:76
  5.3 3.1 %collective-permute-start.3 = (f32[392,768]{1,0:T(8,128)S(1)}, f32[392,768]{1,0:T(8,128)S(1)}, u32[]{:S(2)}, u32[]{:S(2)}) collective-permute-start(f32[392,768]{1,0:T(8,128)S(1)} %get-tuple-element.38.a_ref), channel_id=1, source_target_pairs={{0,8},{2,10},{4,12},{6,14},{8,16},{10,18},{12,20},{14,22},{16,24},... | collective-permute-start | bytes 3612680 | tf_op jit(solution)/shard_map/ppermute | solution.py:296
  8.4 1.5 %collective-permute-start.1 = (f32[392,768]{1,0:T(8,128)S(1)}, f32[392,768]{1,0:T(8,128)S(1)}, u32[]{:S(2)}, u32[]{:S(2)}) collective-permute-start(f32[392,768]{1,0:T(8,128)S(1)} %get-tuple-element.38.a_ref), channel_id=1, source_target_pairs={{0,4},{2,6},{4,0},{6,2},{8,12},{10,14},{12,8},{14,10},{16,20},{18,... | collective-permute-start | bytes 3612680 | tf_op jit(solution)/shard_map/ppermute | solution.py:290
  9.9 1.5 %collective-permute-start = (f32[392,768]{1,0:T(8,128)S(1)}, f32[392,768]{1,0:T(8,128)S(1)}, u32[]{:S(2)}, u32[]{:S(2)}) collective-permute-start(f32[392,768]{1,0:T(8,128)S(1)} %get-tuple-element.38.a_ref), channel_id=1, source_target_pairs={{0,1},{1,0},{2,3},{3,2},{4,5},{5,4},{6,7},{7,6},{8,9},{9,8},{10,11... | collective-permute-start | bytes 3612680 | tf_op jit(solution)/shard_map/ppermute | solution.py:287
  11.4 2.2 %collective-permute-start.4 = (f32[136,768]{1,0:T(8,128)S(1)}, f32[136,768]{1,0:T(8,128)S(1)}, u32[]{:S(2)}, u32[]{:S(2)}) collective-permute-start(f32[136,768]{1,0:T(8,128)S(1)} %get-tuple-element.40.a_ref), channel_id=1, source_target_pairs={{8,0},{10,2},{12,4},{14,6},{16,8},{18,10},{20,12},{22,14},{24,16},... | collective-permute-start | bytes 1253384 | tf_op jit(solution)/shard_map/ppermute | solution.py:299
  13.6 32.2 %collective-permute-done.4.refs_2_.b_ref = f32[136,768]{1,0:T(8,128)S(1)} collective-permute-done((f32[136,768]{1,0:T(8,128)S(1)}, f32[136,768]{1,0:T(8,128)S(1)}, u32[]{:S(2)}, u32[]{:S(2)}) %collective-permute-start.4) | collective-permute-done | bytes 417824 | tf_op jit(solution)/shard_map/ppermute | solution.py:299
  45.9 0.1 cut.1
  45.9 0.6 choose.7
  46.6 1.6 %collective-permute-start.8 = (f32[136,768]{1,0:T(8,128)S(1)}, f32[136,768]{1,0:T(8,128)S(1)}, u32[]{:S(2)}, u32[]{:S(2)}) collective-permute-start(f32[136,768]{1,0:T(8,128)S(1)} %get-tuple-element.46), channel_id=1, source_target_pairs={{0,1},{1,0},{2,3},{3,2},{4,5},{5,4},{6,7},{7,6},{8,9},{9,8},{10,11... | collective-permute-start | bytes 1253384 | tf_op jit(solution)/shard_map/ppermute | solution.py:287
  48.1 1.4 collective-permute-start.2
  49.6 1.8 %collective-permute-start.20 = (f32[128,768]{1,0:T(8,128)S(1)}, f32[128,768]{1,0:T(8,128)S(1)}, u32[]{:S(2)}, u32[]{:S(2)}) collective-permute-start(f32[128,768]{1,0:T(8,128)S(1)} %get-tuple-element.55.a_ref), channel_id=1, source_target_pairs={{8,0},{10,2},{12,4},{14,6},{16,8},{18,10},{20,12},{22,14},{24,16},... | collective-permute-start | bytes 1179656 | tf_op jit(solution)/shard_map/ppermute | solution.py:299
  51.4 6.8 %collective-permute-done.8.b_ref.refs_3_.refs_6_ = f32[136,768]{1,0:T(8,128)S(1)} collective-permute-done((f32[136,768]{1,0:T(8,128)S(1)}, f32[136,768]{1,0:T(8,128)S(1)}, u32[]{:S(2)}, u32[]{:S(2)}) %collective-permute-start.8) | collective-permute-done | bytes 417824 | tf_op jit(solution)/shard_map/ppermute | solution.py:287
  58.1 0.1 pair.6
  58.2 0.1 collective-permute-start.9
  58.3 0.6 collective-permute-start.6
  58.9 1.0 collective-permute-done.20.b_ref
  59.9 0.6 choose.10
  60.5 0.8 collective-permute-start.21
  61.3 8.5 %collective-permute-done.6.b_ref = f32[128,768]{1,0:T(8,128)S(1)} collective-permute-done((f32[128,768]{1,0:T(8,128)S(1)}, f32[128,768]{1,0:T(8,128)S(1)}, u32[]{:S(2)}, u32[]{:S(2)}) %collective-permute-start.6) | collective-permute-done | bytes 393248 | tf_op jit(solution)/shard_map/ppermute | solution.py:299
  69.8 0.6 choose.6
  70.4 1.6 %collective-permute-start.7 = (f32[128,768]{1,0:T(8,128)S(1)}, f32[128,768]{1,0:T(8,128)S(1)}, u32[]{:S(2)}, u32[]{:S(2)}) collective-permute-start(f32[128,768]{1,0:T(8,128)S(1)} %get-tuple-element.43), channel_id=1, source_target_pairs={{0,1},{1,0},{2,3},{3,2},{4,5},{5,4},{6,7},{7,6},{8,9},{9,8},{10,11... | collective-permute-start | bytes 1179656 | tf_op jit(solution)/shard_map/ppermute | solution.py:287
  72.0 0.1 collective-permute-start.22
  72.1 0.7 collective-permute-start.14
  72.8 0.8 unit_rows.2.refs_0_
  73.5 2.7 %collective-permute-done.2.b_ref.refs_1_ = f32[392,768]{1,0:T(8,128)S(1)} collective-permute-done((f32[392,768]{1,0:T(8,128)S(1)}, f32[392,768]{1,0:T(8,128)S(1)}, u32[]{:S(2)}, u32[]{:S(2)}) %collective-permute-start.2) | collective-permute-done | bytes 1204256 | tf_op jit(solution)/shard_map/ppermute | solution.py:290
  76.2 0.8 unit_rows.3.refs_1_
  77.0 2.2 %product.6 = (f32[384,256]{1,0:T(8,128)S(1)}, f32[384,256]{1,0:T(8,128)S(1)}) custom-call(bf16[768,1536]{1,0:T(8,128)(2,1)S(1)} %unit_rows.2.refs_0_, bf16[768,1536]{1,0:T(8,128)(2,1)S(1)} %unit_rows.3.refs_1_, f32[136,768]{1,0:T(8,128)S(1)} %get-tuple-element.45.a_ref.refs_2_.refs_5_, f32[136,768]{1,0:T(8,128)S(1)} %collective-permute-done.8.b_ref.refs_3_.refs_6_, ...), custom_call_target="tpu_custom_call" | custom-call | flops 1 | bytes 1 | tf_op jit(solution)/shard_map/product/pallas_call | solution.py:229
  79.2 1.9 %collective-permute-done.7.b_ref.refs_3_ = f32[128,768]{1,0:T(8,128)S(1)} collective-permute-done((f32[128,768]{1,0:T(8,128)S(1)}, f32[128,768]{1,0:T(8,128)S(1)}, u32[]{:S(2)}, u32[]{:S(2)}) %collective-permute-start.7) | collective-permute-done | bytes 393248 | tf_op jit(solution)/shard_map/ppermute | solution.py:287
  81.2 0.1 collective-permute-start.10
  81.3 0.7 collective-permute-start.19
  81.9 1.5 %collective-permute-start.16 = (f32[384,256]{1,0:T(8,128)S(1)}, f32[384,256]{1,0:T(8,128)S(1)}, u32[]{:S(2)}, u32[]{:S(2)}) collective-permute-start(f32[384,256]{1,0:T(8,128)S(1)} %get-tuple-element.47.refs_0_.refs_8_), channel_id=1, source_target_pairs={{0,4},{2,6},{4,0},{6,2},{8,12},{10,14},{12,8},{14,10},{16,20},{18,... | collective-permute-start | bytes 1179656 | tf_op jit(solution)/shard_map/ppermute | solution.py:290
  83.5 2.5 %collective-permute-done.14.b_ref = f32[136,768]{1,0:T(8,128)S(1)} collective-permute-done((f32[136,768]{1,0:T(8,128)S(1)}, f32[136,768]{1,0:T(8,128)S(1)}, u32[]{:S(2)}, u32[]{:S(2)}) %collective-permute-start.14) | collective-permute-done | bytes 417824 | tf_op jit(solution)/shard_map/ppermute | solution.py:296
  85.9 0.6 choose.9
  86.6 0.6 collective-permute-start.15
  87.2 2.2 %product.9 = (f32[384,256]{1,0:T(8,128)S(1)}, f32[384,256]{1,0:T(8,128)S(1)}) custom-call(bf16[768,1536]{1,0:T(8,128)(2,1)S(1)} %unit_rows.2.refs_0_, bf16[768,1536]{1,0:T(8,128)(2,1)S(1)} %unit_rows.3.refs_1_, f32[128,768]{1,0:T(8,128)S(1)} %get-tuple-element.57.a_ref.refs_2_, f32[128,768]{1,0:T(8,128)S(1)} %collective-permute-done.21.b_ref.refs_3_, ...), custom_call_target="tpu_custom_call" | custom-call | flops 1 | bytes 1 | tf_op jit(solution)/shard_map/product/pallas_call | solution.py:229
  89.4 1.6 %collective-permute-start.24 = (f32[384,256]{1,0:T(8,128)S(1)}, f32[384,256]{1,0:T(8,128)S(1)}, u32[]{:S(2)}, u32[]{:S(2)}) collective-permute-start(f32[384,256]{1,0:T(8,128)S(1)} %get-tuple-element.59.refs_0_), channel_id=1, source_target_pairs={{0,4},{2,6},{4,0},{6,2},{8,12},{10,14},{12,8},{14,10},{16,20},{18,... | collective-permute-start | bytes 1179656 | tf_op jit(solution)/shard_map/ppermute | solution.py:290
  91.0 2.2 %product.7 = (f32[384,256]{1,0:T(8,128)S(1)}, f32[384,256]{1,0:T(8,128)S(1)}) custom-call(bf16[768,1536]{1,0:T(8,128)(2,1)S(1)} %unit_rows.2.refs_0_, bf16[768,1536]{1,0:T(8,128)(2,1)S(1)} %unit_rows.3.refs_1_, f32[128,768]{1,0:T(8,128)S(1)} %get-tuple-element.42.a_ref.refs_2_, f32[128,768]{1,0:T(8,128)S(1)} %collective-permute-done.7.b_ref.refs_3_, ...), custom_call_target="tpu_custom_call" | custom-call | flops 1 | bytes 1 | tf_op jit(solution)/shard_map/product/pallas_call | solution.py:229
  93.2 1.8 %collective-permute-done.19.b_ref = f32[128,768]{1,0:T(8,128)S(1)} collective-permute-done((f32[128,768]{1,0:T(8,128)S(1)}, f32[128,768]{1,0:T(8,128)S(1)}, u32[]{:S(2)}, u32[]{:S(2)}) %collective-permute-start.19) | collective-permute-done | bytes 393248 | tf_op jit(solution)/shard_map/ppermute | solution.py:296
  95.0 0.6 choose.11
  95.7 1.6 %collective-permute-start.23 = (f32[128,768]{1,0:T(8,128)S(1)}, f32[128,768]{1,0:T(8,128)S(1)}, u32[]{:S(2)}, u32[]{:S(2)}) collective-permute-start(f32[128,768]{1,0:T(8,128)S(1)} %get-tuple-element.61), channel_id=1, source_target_pairs={{0,1},{1,0},{2,3},{3,2},{4,5},{5,4},{6,7},{7,6},{8,9},{9,8},{10,11... | collective-permute-start | bytes 1179656 | tf_op jit(solution)/shard_map/ppermute | solution.py:287
  97.2 5.8 %collective-permute-done.5.b_ref = f32[128,768]{1,0:T(8,128)S(1)} collective-permute-done((f32[128,768]{1,0:T(8,128)S(1)}, f32[128,768]{1,0:T(8,128)S(1)}, u32[]{:S(2)}, u32[]{:S(2)}) %collective-permute-start.5) | collective-permute-done | bytes 393248 | tf_op jit(solution)/shard_map/ppermute | solution.py:296
  103.0 0.6 choose.8
  103.6 1.6 %collective-permute-start.11 = (f32[128,768]{1,0:T(8,128)S(1)}, f32[128,768]{1,0:T(8,128)S(1)}, u32[]{:S(2)}, u32[]{:S(2)}) collective-permute-start(f32[128,768]{1,0:T(8,128)S(1)} %get-tuple-element.50), channel_id=1, source_target_pairs={{0,1},{1,0},{2,3},{3,2},{4,5},{5,4},{6,7},{7,6},{8,9},{9,8},{10,11... | collective-permute-start | bytes 1179656 | tf_op jit(solution)/shard_map/ppermute | solution.py:287
  105.2 1.3 collective-permute-start.12
  106.6 0.1 collective-permute-start.17
  106.8 0.5 collective-permute-start.25
  107.3 7.4 %collective-permute-done.11.b_ref.refs_3_ = f32[128,768]{1,0:T(8,128)S(1)} collective-permute-done((f32[128,768]{1,0:T(8,128)S(1)}, f32[128,768]{1,0:T(8,128)S(1)}, u32[]{:S(2)}, u32[]{:S(2)}) %collective-permute-start.11) | collective-permute-done | bytes 393248 | tf_op jit(solution)/shard_map/ppermute | solution.py:287
  114.7 0.9 collective-permute-done.12.refs_0_.refs_5_
  115.6 0.1 collective-permute-start.13
  115.7 2.2 %product.11 = (f32[384,256]{1,0:T(8,128)S(1)}, f32[384,256]{1,0:T(8,128)S(1)}) custom-call(bf16[768,1536]{1,0:T(8,128)(2,1)S(1)} %unit_rows.2.refs_0_, bf16[768,1536]{1,0:T(8,128)(2,1)S(1)} %unit_rows.3.refs_1_, f32[136,768]{1,0:T(8,128)S(1)} %get-tuple-element.51.a_ref.refs_5_.refs_2_, f32[136,768]{1,0:T(8,128)S(1)} %collective-permute-done.15.b_ref.refs_6_.refs_3_, ...), custom_call_target="tpu_custom_call" | custom-call | flops 1 | bytes 1 | tf_op jit(solution)/shard_map/product/pallas_call | solution.py:229
  118.0 1.4 collective-permute-start.27
  119.4 2.2 %product.10 = (f32[384,256]{1,0:T(8,128)S(1)}, f32[384,256]{1,0:T(8,128)S(1)}) custom-call(bf16[768,1536]{1,0:T(8,128)(2,1)S(1)} %unit_rows.2.refs_0_, bf16[768,1536]{1,0:T(8,128)(2,1)S(1)} %unit_rows.3.refs_1_, f32[128,768]{1,0:T(8,128)S(1)} %get-tuple-element.60.a_ref.refs_2_, f32[128,768]{1,0:T(8,128)S(1)} %collective-permute-done.23.b_ref.refs_3_, ...), custom_call_target="tpu_custom_call" | custom-call | flops 1 | bytes 1 | tf_op jit(solution)/shard_map/product/pallas_call | solution.py:229
  121.6 0.7 collective-permute-start.26
  122.4 2.2 %product.8 = (f32[384,256]{1,0:T(8,128)S(1)}, f32[384,256]{1,0:T(8,128)S(1)}) custom-call(bf16[768,1536]{1,0:T(8,128)(2,1)S(1)} %unit_rows.2.refs_0_, bf16[768,1536]{1,0:T(8,128)(2,1)S(1)} %unit_rows.3.refs_1_, f32[128,768]{1,0:T(8,128)S(1)} %get-tuple-element.49.a_ref.refs_2_, f32[128,768]{1,0:T(8,128)S(1)} %collective-permute-done.11.b_ref.refs_3_, ...), custom_call_target="tpu_custom_call" | custom-call | flops 1 | bytes 1 | tf_op jit(solution)/shard_map/product/pallas_call | solution.py:229
  124.6 1.4 collective-permute-start.18
  126.0 2.8 %place.4.refs_2_ = f32[384,3072]{1,0:T(8,128)} custom-call(s32[10]{0:T(128)S(1)} %get-tuple-element.37.first_ref.at_ref, f32[384,256]{1,0:T(8,128)S(1)} %get-tuple-element.66.refs_0_, f32[384,256]{1,0:T(8,128)S(1)} %get-tuple-element.67.refs_1_, f32[384,256]{1,0:T(8,128)S(1)} %get-tuple-element.68.refs_2_, ...), custom_call_target="tpu_custom_call" | custom-call | flops 1 | bytes 1 | tf_op jit(solution)/shard_map/place/pallas_call | solution.py:264
  128.8 1.1 collective-permute-done.27.refs_1_
  129.9 2.1 %place.5.refs_2_ = f32[384,3072]{1,0:T(8,128)} custom-call(s32[10]{0:T(128)S(1)} %get-tuple-element.37.first_ref.at_ref, f32[384,256]{1,0:T(8,128)S(1)} %get-tuple-element.64.refs_0_, f32[384,256]{1,0:T(8,128)S(1)} %collective-permute-done.27.refs_1_, f32[384,3072]{1,0:T(8,128)} %place.4.refs_2_), custom_call_target="tpu_custom_call", output_to_operand_aliasing={{}: (3, {})} | custom-call | flops 1 | bytes 1 | tf_op jit(solution)/shard_map/place/pallas_call | solution.py:264
  132.1 6.3 %collective-permute-done.26.refs_1_ = f32[384,256]{1,0:T(8,128)S(1)} collective-permute-done((f32[384,256]{1,0:T(8,128)S(1)}, f32[384,256]{1,0:T(8,128)S(1)}, u32[]{:S(2)}, u32[]{:S(2)}) %collective-permute-start.26) | collective-permute-done | bytes 393248 | tf_op jit(solution)/shard_map/ppermute | solution.py:290
  138.4 2.2 %place.6.refs_2_ = f32[384,3072]{1,0:T(8,128)} custom-call(s32[10]{0:T(128)S(1)} %get-tuple-element.37.first_ref.at_ref, f32[384,256]{1,0:T(8,128)S(1)} %get-tuple-element.62.refs_0_, f32[384,256]{1,0:T(8,128)S(1)} %collective-permute-done.26.refs_1_, f32[384,3072]{1,0:T(8,128)} %place.5.refs_2_), custom_call_target="tpu_custom_call", output_to_operand_aliasing={{}: (3, {})} | custom-call | flops 1 | bytes 1 | tf_op jit(solution)/shard_map/place/pallas_call | solution.py:264
  140.5 5.9 %collective-permute-done.18.refs_1_ = f32[384,256]{1,0:T(8,128)S(1)} collective-permute-done((f32[384,256]{1,0:T(8,128)S(1)}, f32[384,256]{1,0:T(8,128)S(1)}, u32[]{:S(2)}, u32[]{:S(2)}) %collective-permute-start.18) | collective-permute-done | bytes 393248 | tf_op jit(solution)/shard_map/ppermute | solution.py:290
  146.4 2.2 %place.7 = f32[384,3072]{1,0:T(8,128)} custom-call(s32[10]{0:T(128)S(1)} %get-tuple-element.37.first_ref.at_ref, f32[384,256]{1,0:T(8,128)S(1)} %get-tuple-element.53.refs_0_, f32[384,256]{1,0:T(8,128)S(1)} %collective-permute-done.18.refs_1_, f32[384,3072]{1,0:T(8,128)} %place.6.refs_2_), custom_call_target="tpu_custom_call", output_to_operand_aliasing={{}: (3, {})} | custom-call | flops 1 | bytes 1 | tf_op jit(solution)/shard_map/place/pallas_call | solution.py:264
  (22 shorter events, 0.3 us)
Async XLA Ops:
  0.0 1.7 %copy-start = (f32[384,1536]{1,0:T(8,128)S(1)}, f32[384,1536]{1,0:T(8,128)}, u32[]{:S(2)}) copy-start(f32[384,1536]{1,0:T(8,128)} %library_ref.1) | copy-start | bytes 7077892
  1.7 0.7 copy-start.1
  5.3 40.6 %collective-permute-start.3 = (f32[392,768]{1,0:T(8,128)S(1)}, f32[392,768]{1,0:T(8,128)S(1)}, u32[]{:S(2)}, u32[]{:S(2)}) collective-permute-start(f32[392,768]{1,0:T(8,128)S(1)} %get-tuple-element.38.a_ref), channel_id=1, source_target_pairs={{0,8},{2,10},{4,12},{6,14},{8,16},{10,18},{12,20},{14,22},{16,24},... | collective-permute-start | bytes 3612680 | tf_op jit(solution)/shard_map/ppermute | solution.py:296
  8.4 37.5 %collective-permute-start.1 = (f32[392,768]{1,0:T(8,128)S(1)}, f32[392,768]{1,0:T(8,128)S(1)}, u32[]{:S(2)}, u32[]{:S(2)}) collective-permute-start(f32[392,768]{1,0:T(8,128)S(1)} %get-tuple-element.38.a_ref), channel_id=1, source_target_pairs={{0,4},{2,6},{4,0},{6,2},{8,12},{10,14},{12,8},{14,10},{16,20},{18,... | collective-permute-start | bytes 3612680 | tf_op jit(solution)/shard_map/ppermute | solution.py:290
  9.9 36.0 %collective-permute-start = (f32[392,768]{1,0:T(8,128)S(1)}, f32[392,768]{1,0:T(8,128)S(1)}, u32[]{:S(2)}, u32[]{:S(2)}) collective-permute-start(f32[392,768]{1,0:T(8,128)S(1)} %get-tuple-element.38.a_ref), channel_id=1, source_target_pairs={{0,1},{1,0},{2,3},{3,2},{4,5},{5,4},{6,7},{7,6},{8,9},{9,8},{10,11... | collective-permute-start | bytes 3612680 | tf_op jit(solution)/shard_map/ppermute | solution.py:287
  11.4 34.5 %collective-permute-start.4 = (f32[136,768]{1,0:T(8,128)S(1)}, f32[136,768]{1,0:T(8,128)S(1)}, u32[]{:S(2)}, u32[]{:S(2)}) collective-permute-start(f32[136,768]{1,0:T(8,128)S(1)} %get-tuple-element.40.a_ref), channel_id=1, source_target_pairs={{8,0},{10,2},{12,4},{14,6},{16,8},{18,10},{20,12},{22,14},{24,16},... | collective-permute-start | bytes 1253384 | tf_op jit(solution)/shard_map/ppermute | solution.py:299
  46.6 11.6 %collective-permute-start.8 = (f32[136,768]{1,0:T(8,128)S(1)}, f32[136,768]{1,0:T(8,128)S(1)}, u32[]{:S(2)}, u32[]{:S(2)}) collective-permute-start(f32[136,768]{1,0:T(8,128)S(1)} %get-tuple-element.46), channel_id=1, source_target_pairs={{0,1},{1,0},{2,3},{3,2},{4,5},{5,4},{6,7},{7,6},{8,9},{9,8},{10,11... | collective-permute-start | bytes 1253384 | tf_op jit(solution)/shard_map/ppermute | solution.py:287
  48.1 28.1 %collective-permute-start.2 = (f32[392,768]{1,0:T(8,128)S(1)}, f32[392,768]{1,0:T(8,128)S(1)}, u32[]{:S(2)}, u32[]{:S(2)}) collective-permute-start(f32[392,768]{1,0:T(8,128)S(1)} %collective-permute-done.b_ref.refs_0_), channel_id=1, source_target_pairs={{0,4},{2,6},{4,0},{6,2},{8,12},{10,14},{12,8},{14,10},{16,20},{18,... | collective-permute-start | bytes 3612680 | tf_op jit(solution)/shard_map/ppermute | solution.py:290
  49.6 10.3 %collective-permute-start.20 = (f32[128,768]{1,0:T(8,128)S(1)}, f32[128,768]{1,0:T(8,128)S(1)}, u32[]{:S(2)}, u32[]{:S(2)}) collective-permute-start(f32[128,768]{1,0:T(8,128)S(1)} %get-tuple-element.55.a_ref), channel_id=1, source_target_pairs={{8,0},{10,2},{12,4},{14,6},{16,8},{18,10},{20,12},{22,14},{24,16},... | collective-permute-start | bytes 1179656 | tf_op jit(solution)/shard_map/ppermute | solution.py:299
  58.2 18.8 %collective-permute-start.9 = (f32[2,136,768]{2,1,0:T(8,128)S(1)}, f32[2,136,768]{2,1,0:T(8,128)S(1)}, u32[]{:S(2)}, u32[]{:S(2)}) collective-permute-start(f32[2,136,768]{2,1,0:T(8,128)S(1)} %pair.6), channel_id=1, source_target_pairs={{0,2},{2,0},{4,6},{6,4},{8,10},{10,8},{12,14},{14,12},{16,18},{18,... | collective-permute-start | bytes 2506760 | tf_op jit(solution)/shard_map/ppermute | solution.py:293
  58.3 11.5 %collective-permute-start.6 = (f32[128,768]{1,0:T(8,128)S(1)}, f32[128,768]{1,0:T(8,128)S(1)}, u32[]{:S(2)}, u32[]{:S(2)}) collective-permute-start(f32[128,768]{1,0:T(8,128)S(1)} %get-tuple-element.39.a_ref), channel_id=1, source_target_pairs={{8,0},{10,2},{12,4},{14,6},{16,8},{18,10},{20,12},{22,14},{24,16},... | collective-permute-start | bytes 1179656 | tf_op jit(solution)/shard_map/ppermute | solution.py:299
  60.5 11.5 %collective-permute-start.21 = (f32[128,768]{1,0:T(8,128)S(1)}, f32[128,768]{1,0:T(8,128)S(1)}, u32[]{:S(2)}, u32[]{:S(2)}) collective-permute-start(f32[128,768]{1,0:T(8,128)S(1)} %get-tuple-element.58), channel_id=1, source_target_pairs={{0,1},{1,0},{2,3},{3,2},{4,5},{5,4},{6,7},{7,6},{8,9},{9,8},{10,11... | collective-permute-start | bytes 1179656 | tf_op jit(solution)/shard_map/ppermute | solution.py:287
  70.4 10.7 %collective-permute-start.7 = (f32[128,768]{1,0:T(8,128)S(1)}, f32[128,768]{1,0:T(8,128)S(1)}, u32[]{:S(2)}, u32[]{:S(2)}) collective-permute-start(f32[128,768]{1,0:T(8,128)S(1)} %get-tuple-element.43), channel_id=1, source_target_pairs={{0,1},{1,0},{2,3},{3,2},{4,5},{5,4},{6,7},{7,6},{8,9},{9,8},{10,11... | collective-permute-start | bytes 1179656 | tf_op jit(solution)/shard_map/ppermute | solution.py:287
  72.0 14.5 %collective-permute-start.22 = (f32[2,128,768]{2,1,0:T(8,128)S(1)}, f32[2,128,768]{2,1,0:T(8,128)S(1)}, u32[]{:S(2)}, u32[]{:S(2)}) collective-permute-start(f32[2,128,768]{2,1,0:T(8,128)S(1)} %pair.10), channel_id=1, source_target_pairs={{0,2},{2,0},{4,6},{6,4},{8,10},{10,8},{12,14},{14,12},{16,18},{18,... | collective-permute-start | bytes 2359304 | tf_op jit(solution)/shard_map/ppermute | solution.py:293
  72.1 13.8 %collective-permute-start.14 = (f32[136,768]{1,0:T(8,128)S(1)}, f32[136,768]{1,0:T(8,128)S(1)}, u32[]{:S(2)}, u32[]{:S(2)}) collective-permute-start(f32[136,768]{1,0:T(8,128)S(1)} %get-tuple-element.44.a_ref), channel_id=1, source_target_pairs={{0,8},{2,10},{4,12},{6,14},{8,16},{10,18},{12,20},{14,22},{16,24},... | collective-permute-start | bytes 1253384 | tf_op jit(solution)/shard_map/ppermute | solution.py:296
  81.2 8.2 %collective-permute-start.10 = (f32[2,128,768]{2,1,0:T(8,128)S(1)}, f32[2,128,768]{2,1,0:T(8,128)S(1)}, u32[]{:S(2)}, u32[]{:S(2)}) collective-permute-start(f32[2,128,768]{2,1,0:T(8,128)S(1)} %pair.7), channel_id=1, source_target_pairs={{0,2},{2,0},{4,6},{6,4},{8,10},{10,8},{12,14},{14,12},{16,18},{18,... | collective-permute-start | bytes 2359304 | tf_op jit(solution)/shard_map/ppermute | solution.py:293
  81.3 13.8 %collective-permute-start.19 = (f32[128,768]{1,0:T(8,128)S(1)}, f32[128,768]{1,0:T(8,128)S(1)}, u32[]{:S(2)}, u32[]{:S(2)}) collective-permute-start(f32[128,768]{1,0:T(8,128)S(1)} %get-tuple-element.56.a_ref), channel_id=1, source_target_pairs={{0,8},{2,10},{4,12},{6,14},{8,16},{10,18},{12,20},{14,22},{16,24},... | collective-permute-start | bytes 1179656 | tf_op jit(solution)/shard_map/ppermute | solution.py:296
  81.9 13.1 %collective-permute-start.16 = (f32[384,256]{1,0:T(8,128)S(1)}, f32[384,256]{1,0:T(8,128)S(1)}, u32[]{:S(2)}, u32[]{:S(2)}) collective-permute-start(f32[384,256]{1,0:T(8,128)S(1)} %get-tuple-element.47.refs_0_.refs_8_), channel_id=1, source_target_pairs={{0,4},{2,6},{4,0},{6,2},{8,12},{10,14},{12,8},{14,10},{16,20},{18,... | collective-permute-start | bytes 1179656 | tf_op jit(solution)/shard_map/ppermute | solution.py:290
  85.9 17.1 %collective-permute-start.5 = (f32[128,768]{1,0:T(8,128)S(1)}, f32[128,768]{1,0:T(8,128)S(1)}, u32[]{:S(2)}, u32[]{:S(2)}) collective-permute-start(f32[128,768]{1,0:T(8,128)S(1)} %get-tuple-element.41.a_ref), channel_id=1, source_target_pairs={{0,8},{2,10},{4,12},{6,14},{8,16},{10,18},{12,20},{14,22},{16,24},... | collective-permute-start | bytes 1179656 | tf_op jit(solution)/shard_map/ppermute | solution.py:296
  86.6 20.0 %collective-permute-start.15 = (f32[136,768]{1,0:T(8,128)S(1)}, f32[136,768]{1,0:T(8,128)S(1)}, u32[]{:S(2)}, u32[]{:S(2)}) collective-permute-start(f32[136,768]{1,0:T(8,128)S(1)} %get-tuple-element.52), channel_id=1, source_target_pairs={{0,1},{1,0},{2,3},{3,2},{4,5},{5,4},{6,7},{7,6},{8,9},{9,8},{10,11... | collective-permute-start | bytes 1253384 | tf_op jit(solution)/shard_map/ppermute | solution.py:287
  89.4 17.3 %collective-permute-start.24 = (f32[384,256]{1,0:T(8,128)S(1)}, f32[384,256]{1,0:T(8,128)S(1)}, u32[]{:S(2)}, u32[]{:S(2)}) collective-permute-start(f32[384,256]{1,0:T(8,128)S(1)} %get-tuple-element.59.refs_0_), channel_id=1, source_target_pairs={{0,4},{2,6},{4,0},{6,2},{8,12},{10,14},{12,8},{14,10},{16,20},{18,... | collective-permute-start | bytes 1179656 | tf_op jit(solution)/shard_map/ppermute | solution.py:290
  95.7 11.0 %collective-permute-start.23 = (f32[128,768]{1,0:T(8,128)S(1)}, f32[128,768]{1,0:T(8,128)S(1)}, u32[]{:S(2)}, u32[]{:S(2)}) collective-permute-start(f32[128,768]{1,0:T(8,128)S(1)} %get-tuple-element.61), channel_id=1, source_target_pairs={{0,1},{1,0},{2,3},{3,2},{4,5},{5,4},{6,7},{7,6},{8,9},{9,8},{10,11... | collective-permute-start | bytes 1179656 | tf_op jit(solution)/shard_map/ppermute | solution.py:287
  103.6 11.1 %collective-permute-start.11 = (f32[128,768]{1,0:T(8,128)S(1)}, f32[128,768]{1,0:T(8,128)S(1)}, u32[]{:S(2)}, u32[]{:S(2)}) collective-permute-start(f32[128,768]{1,0:T(8,128)S(1)} %get-tuple-element.50), channel_id=1, source_target_pairs={{0,1},{1,0},{2,3},{3,2},{4,5},{5,4},{6,7},{7,6},{8,9},{9,8},{10,11... | collective-permute-start | bytes 1179656 | tf_op jit(solution)/shard_map/ppermute | solution.py:287
  105.2 10.4 %collective-permute-start.12 = (f32[384,256]{1,0:T(8,128)S(1)}, f32[384,256]{1,0:T(8,128)S(1)}, u32[]{:S(2)}, u32[]{:S(2)}) collective-permute-start(f32[384,256]{1,0:T(8,128)S(1)} %get-tuple-element.48.refs_0_.refs_2_), channel_id=1, source_target_pairs={{0,4},{2,6},{4,0},{6,2},{8,12},{10,14},{12,8},{14,10},{16,20},{18,... | collective-permute-start | bytes 1179656 | tf_op jit(solution)/shard_map/ppermute | solution.py:290
  106.6 9.1 %collective-permute-start.17 = (f32[2,136,768]{2,1,0:T(8,128)S(1)}, f32[2,136,768]{2,1,0:T(8,128)S(1)}, u32[]{:S(2)}, u32[]{:S(2)}) collective-permute-start(f32[2,136,768]{2,1,0:T(8,128)S(1)} %pair.9), channel_id=1, source_target_pairs={{0,2},{2,0},{4,6},{6,4},{8,10},{10,8},{12,14},{14,12},{16,18},{18,... | collective-permute-start | bytes 2506760 | tf_op jit(solution)/shard_map/ppermute | solution.py:293
  106.8 12.6 %collective-permute-start.25 = (f32[2,128,768]{2,1,0:T(8,128)S(1)}, f32[2,128,768]{2,1,0:T(8,128)S(1)}, u32[]{:S(2)}, u32[]{:S(2)}) collective-permute-start(f32[2,128,768]{2,1,0:T(8,128)S(1)} %pair.11), channel_id=1, source_target_pairs={{0,2},{2,0},{4,6},{6,4},{8,10},{10,8},{12,14},{14,12},{16,18},{18,... | collective-permute-start | bytes 2359304 | tf_op jit(solution)/shard_map/ppermute | solution.py:293
  115.6 6.7 %collective-permute-start.13 = (f32[2,128,768]{2,1,0:T(8,128)S(1)}, f32[2,128,768]{2,1,0:T(8,128)S(1)}, u32[]{:S(2)}, u32[]{:S(2)}) collective-permute-start(f32[2,128,768]{2,1,0:T(8,128)S(1)} %pair.8), channel_id=1, source_target_pairs={{0,2},{2,0},{4,6},{6,4},{8,10},{10,8},{12,14},{14,12},{16,18},{18,... | collective-permute-start | bytes 2359304 | tf_op jit(solution)/shard_map/ppermute | solution.py:293
  118.0 12.0 %collective-permute-start.27 = (f32[384,256]{1,0:T(8,128)S(1)}, f32[384,256]{1,0:T(8,128)S(1)}, u32[]{:S(2)}, u32[]{:S(2)}) collective-permute-start(f32[384,256]{1,0:T(8,128)S(1)} %get-tuple-element.65), channel_id=1, source_target_pairs={{0,4},{2,6},{4,0},{6,2},{8,12},{10,14},{12,8},{14,10},{16,20},{18,... | collective-permute-start | bytes 1179656 | tf_op jit(solution)/shard_map/ppermute | solution.py:290
  121.6 16.7 %collective-permute-start.26 = (f32[384,256]{1,0:T(8,128)S(1)}, f32[384,256]{1,0:T(8,128)S(1)}, u32[]{:S(2)}, u32[]{:S(2)}) collective-permute-start(f32[384,256]{1,0:T(8,128)S(1)} %get-tuple-element.63), channel_id=1, source_target_pairs={{0,4},{2,6},{4,0},{6,2},{8,12},{10,14},{12,8},{14,10},{16,20},{18,... | collective-permute-start | bytes 1179656 | tf_op jit(solution)/shard_map/ppermute | solution.py:290
  124.6 21.8 %collective-permute-start.18 = (f32[384,256]{1,0:T(8,128)S(1)}, f32[384,256]{1,0:T(8,128)S(1)}, u32[]{:S(2)}, u32[]{:S(2)}) collective-permute-start(f32[384,256]{1,0:T(8,128)S(1)} %get-tuple-element.54), channel_id=1, source_target_pairs={{0,4},{2,6},{4,0},{6,2},{8,12},{10,14},{12,8},{14,10},{16,20},{18,... | collective-permute-start | bytes 1179656 | tf_op jit(solution)/shard_map/ppermute | solution.py:290
